TPU v7x, 32 devices: a whole 2x2x4 slice. The times are simulated.
32 devices in a mesh: rep: 1, seq: 8 (over z, y), head: 2 (over x), sub: 2 (over core).
Axes of the slice: x: 2, y: 2, z: 4, core: 2. Of those that a mesh axis runs over, the one named last changes fastest.
Arguments:
- head_query_rows: bfloat16 [2048, 2048], P(('rep', 'seq', 'sub'), 'head'), may hold values from -6 to 6, as said below
- head_key_rows: bfloat16 [2048, 2048], P(('rep', 'seq', 'sub'), 'head'), may hold values from -6 to 6, as said below
- head_value_rows: bfloat16 [2048, 2048], P(('rep', 'seq', 'sub'), 'head'), may hold values from -6 to 6
- output_gradient: bfloat16 [2048, 4096], P(('rep', 'seq', 'sub'), 'head'), may hold values from -6 to 6
- output_matrix: bfloat16 [2048, 4096], P('head', 'sub'), may hold values from -0.125 to 0.125
- adapter_down_weight: bfloat16 [2048, 16], P('head'), may hold values from -0.125 to 0.125
- adapter_up_weight: bfloat16 [16, 4096], replicated, may hold values from -0.09375 to 0.09375
Outputs:
- query_gradient: bfloat16 [2048, 2048], P(('rep', 'seq', 'sub'), 'head')
- key_gradient: bfloat16 [2048, 2048], P(('rep', 'seq', 'sub'), 'head')
- value_gradient: bfloat16 [2048, 2048], P(('rep', 'seq', 'sub'), 'head')
- adapter_down_gradient: float32 [2048, 16], P(('rep', 'head'))
- adapter_up_gradient: float32 [16, 4096], P('rep', 'head')
Inputs may be any that keep to these rules, and one draw needn't show every extreme that they name: `head_query_rows`: entries of the queries are real values within the range. `head_key_rows`: entries of the keys are real values within the range.
All inputs are finite; a program needn't handle non-finite values.
Results may differ from a plain program's by a relative error of at most 0.029.
Values may be sent and summed in bfloat16 or wider, within the bound.
No kernel may reach another device: no remote copies, remote signals or barrier semaphores. Data moves between devices by JAX's collectives and lax.ppermute only.
A program may use at most 64 MiB of HBM per device.

v0:
```python
import functools
import math

import jax
import jax.numpy as jnp
from jax import lax
from jax.experimental import pallas as pl
from jax.experimental.pallas import tpu as pltpu
from jax.sharding import PartitionSpec as P

HD = 128
GROUP = 2048
TILE = 256
HIDDEN = -1e30
SCALE = HD ** (-0.5)
LOG2_SCALE = SCALE * math.log2(math.e)


def dot_nt(left, right):
    return lax.dot_general(
        left, right, (((1,), (1,)), ((), ())), preferred_element_type=jnp.float32
    )


def dot_nn(left, right):
    return jnp.dot(left, right, preferred_element_type=jnp.float32)


def rows_of(ref, blocks, slot_of, first, count):
    parts = [ref[slot_of(block), first : first + count, :] for block in blocks]
    return jnp.concatenate(parts, axis=0)


def in_either_order(body, scalar_ref, blocks):
    for turn in (0, blocks // 2):
        pl.when(scalar_ref[1] == turn)(
            functools.partial(body, lambda block, turn=turn: (block + turn) % blocks)
        )


def scores_of(sub, keys_own, keys_other, queries, tok):
    def tail_hidden(scores, visible):
        head = scores.shape[0] - TILE
        tail = jnp.where(visible, scores[head:], HIDDEN)
        return tail if head == 0 else jnp.concatenate((scores[:head], tail), axis=0)

    key_at = lax.broadcasted_iota(jnp.int32, (TILE, TILE), 0)
    query_at = lax.broadcasted_iota(jnp.int32, (TILE, TILE), 1)
    own = tail_hidden(dot_nt(keys_own, queries), key_at <= query_at)
    other = tail_hidden(
        dot_nt(keys_other, queries), key_at // tok < query_at // tok + sub
    )
    return own, other


def forward_kernel(tok, scalar_ref, own_ref, *refs):
    body = functools.partial(forward_body, tok, scalar_ref, own_ref, *refs)
    in_either_order(body, scalar_ref, own_ref.shape[0])


def forward_body(
    tok, scalar_ref, own_ref, other_ref, down_t_ref, attn_ref, mid_ref, stat_ref, slot_of
):
    blocks = own_ref.shape[0]
    step = TILE // tok
    sub = scalar_ref[0]
    values_own_t = rows_of(own_ref, range(blocks), slot_of, 2 * tok, tok).T
    values_other_t = rows_of(other_ref, range(blocks), slot_of, tok, tok).T
    for tile in range(blocks // step):
        here = range(tile * step, (tile + 1) * step)
        width = (tile + 1) * TILE
        at = tile * TILE
        upto = range((tile + 1) * step)
        queries = rows_of(own_ref, here, slot_of, 0, tok)
        keys_own = rows_of(own_ref, upto, slot_of, tok, tok)
        keys_other = rows_of(other_ref, upto, slot_of, 0, tok)
        own, other = scores_of(sub, keys_own, keys_other, queries, tok)
        highest = jnp.maximum(
            jnp.max(own, axis=0, keepdims=True), jnp.max(other, axis=0, keepdims=True)
        )
        own = jnp.exp2((own - highest) * LOG2_SCALE)
        other = jnp.exp2((other - highest) * LOG2_SCALE)
        inverse = 1.0 / (
            jnp.sum(own, axis=0, keepdims=True) + jnp.sum(other, axis=0, keepdims=True)
        )
        attn = dot_nn(values_own_t[:, :width], own.astype(jnp.bfloat16)) + dot_nn(
            values_other_t[:, :width], other.astype(jnp.bfloat16)
        )
        attn = (attn * inverse).astype(jnp.bfloat16)
        attn_ref[:, at : at + TILE] = attn
        mid = dot_nn(down_t_ref[...], attn)
        for i, block in enumerate(here):
            mid_ref[slot_of(block)] = mid[:, i * tok : (i + 1) * tok].astype(jnp.bfloat16)
        stat_ref[0:1, at : at + TILE] = highest
        stat_ref[1:2, at : at + TILE] = inverse


def backward_kernel(tok, scalar_ref, own_ref, *refs):
    body = functools.partial(backward_body, tok, scalar_ref, own_ref, *refs)
    in_either_order(body, scalar_ref, own_ref.shape[0])


def backward_body(
    tok,
    scalar_ref,
    own_ref,
    other_ref,
    dout_ref,
    attn_ref,
    stat_ref,
    dq_ref,
    dk_own_ref,
    dv_own_ref,
    pair_other_ref,
    down_grad_ref,
    dk_own,
    dv_own,
    dk_other,
    dv_other,
    slot_of,
):
    blocks = own_ref.shape[0]
    step = TILE // tok
    sub = scalar_ref[0]
    low_rank = down_grad_ref.shape[0]
    keys_own_t = rows_of(own_ref, range(blocks), slot_of, tok, tok).T
    keys_other_t = rows_of(other_ref, range(blocks), slot_of, 0, tok).T
    tiles = blocks // step
    down_total = jnp.zeros((low_rank, HD), jnp.float32)
    for tile in reversed(range(tiles)):
        here = range(tile * step, (tile + 1) * step)
        width = (tile + 1) * TILE
        at = tile * TILE
        queries = rows_of(own_ref, here, slot_of, 0, tok)
        douts_t = jnp.concatenate([dout_ref[slot_of(b), 0:HD, :] for b in here], axis=1)
        highest = stat_ref[0:1, at : at + TILE]
        inverse = stat_ref[1:2, at : at + TILE]
        upto = range((tile + 1) * step)
        keys_own = rows_of(own_ref, upto, slot_of, tok, tok)
        keys_other = rows_of(other_ref, upto, slot_of, 0, tok)
        own, other = scores_of(sub, keys_own, keys_other, queries, tok)
        own = jnp.exp2((own - highest) * LOG2_SCALE) * inverse
        other = jnp.exp2((other - highest) * LOG2_SCALE) * inverse
        dprob_own = dot_nn(rows_of(own_ref, upto, slot_of, 2 * tok, tok), douts_t)
        dprob_other = dot_nn(rows_of(other_ref, upto, slot_of, tok, tok), douts_t)
        delta = jnp.sum(own * dprob_own, axis=0, keepdims=True) + jnp.sum(
            other * dprob_other, axis=0, keepdims=True
        )
        ds_own = (own * (dprob_own - delta)).astype(jnp.bfloat16)
        ds_other = (other * (dprob_other - delta)).astype(jnp.bfloat16)
        dq = dot_nn(keys_own_t[:, :width], ds_own) + dot_nn(keys_other_t[:, :width], ds_other)
        dq = (dq * SCALE).T.astype(jnp.bfloat16)
        terms = (
            (dk_own, dot_nn(ds_own, queries)),
            (dk_other, dot_nn(ds_other, queries)),
            (dv_own, dot_nt(own.astype(jnp.bfloat16), douts_t)),
            (dv_other, dot_nt(other.astype(jnp.bfloat16), douts_t)),
        )
        for total, term in terms:
            if tile == tiles - 1:
                total[...] = term
            else:
                total[0:width] += term
        for i, block in enumerate(here):
            slot = slot_of(block)
            dq_ref[slot] = dq[i * tok : (i + 1) * tok]
            lora = dout_ref[slot, HD : HD + low_rank, :]
            attn = attn_ref[:, at + i * tok : at + (i + 1) * tok]
            down_total += dot_nt(lora, attn)
    for block in range(blocks):
        rows = pl.ds(block * tok, tok)
        slot = slot_of(block)
        dk_own_ref[slot] = dk_own[rows, :] * SCALE
        dv_own_ref[slot] = dv_own[rows, :]
        pair_other_ref[slot, 0:tok, :] = (dk_other[rows, :] * SCALE).astype(jnp.bfloat16)
        pair_other_ref[slot, tok : 2 * tok, :] = dv_other[rows, :].astype(jnp.bfloat16)
    down_grad_ref[...] = 2.0 * down_total


def call_kernel(body, outs, scratch, flops, exps, *operands, declared=None, limit=48):
    in_bytes = sum(x.size * x.dtype.itemsize for x in operands)
    out_bytes = sum(x.size * x.dtype.itemsize for x in outs)
    specs = [pl.BlockSpec(memory_space=pltpu.SMEM)]
    specs += [pl.BlockSpec(memory_space=pltpu.VMEM)] * (len(operands) - 1)
    return pl.pallas_call(
        body,
        out_shape=outs,
        in_specs=specs,
        out_specs=[pl.BlockSpec(memory_space=pltpu.VMEM)] * len(outs),
        scratch_shapes=scratch,
        compiler_params=pltpu.CompilerParams(vmem_limit_bytes=limit * 1024 * 1024),
        cost_estimate=pl.CostEstimate(
            flops=flops,
            bytes_accessed=declared or in_bytes + out_bytes,
            transcendentals=exps,
        ),
    )(*operands)


def shape_of(shape, dtype):
    return jax.ShapeDtypeStruct(shape, dtype)


def butterfly_sum(value, axis, bits, count):
    for bit in bits:
        pairs = [(i, i ^ bit) for i in range(count)]
        value = value.astype(jnp.bfloat16)
        taken = lax.ppermute(value, axis, pairs)
        value = value.astype(jnp.float32) + taken.astype(jnp.float32)
    return value


def powers_below(count):
    return [1 << n for n in range(count.bit_length() - 1)]


def message_kernel(copies, *refs):
    count = (len(refs) - 3) // 2
    operands, message_ref = refs[:count], refs[count]
    held, in_sems, out_sems = refs[count + 1 : -2], refs[-2], refs[-1]
    tok = operands[0].shape[0]
    arriving = [
        pltpu.make_async_copy(ref, to, in_sems.at[n])
        for n, (ref, to) in enumerate(zip(operands, held))
    ]
    for copy in arriving:
        copy.start()
    leaving = []
    for n, (copy, ref) in enumerate(zip(arriving, held)):
        copy.wait()
        for rank in range(message_ref.shape[0]):
            cols = pl.ds((rank // copies) * HD, HD)
            to = message_ref.at[rank, pl.ds(n * tok, tok), :]
            leaving.append(pltpu.make_async_copy(ref.at[:, cols], to, out_sems.at[len(leaving)]))
            leaving[-1].start()
    for copy in leaving:
        copy.wait()


def message_of(copies, ranks, *operands):
    tok = operands[0].shape[0]
    count = len(operands)
    shape = (ranks, count * tok, HD)
    return pl.pallas_call(
        functools.partial(message_kernel, copies),
        out_shape=shape_of(shape, operands[0].dtype),
        in_specs=[pl.BlockSpec(memory_space=pltpu.HBM)] * count,
        out_specs=pl.BlockSpec(memory_space=pltpu.HBM),
        scratch_shapes=[pltpu.VMEM(x.shape, x.dtype) for x in operands]
        + [pltpu.SemaphoreType.DMA((count,)), pltpu.SemaphoreType.DMA((ranks * count,))],
        cost_estimate=pl.CostEstimate(
            flops=0, bytes_accessed=4 * math.prod(shape), transcendentals=0
        ),
    )(*operands)


def unpack_kernel(copies, back_ref, *refs):
    out_refs, down_ref = refs[:3], refs[3] if len(refs) > 3 else None
    tok = out_refs[0].shape[0]
    for at_head in range(out_refs[0].shape[1] // HD):
        cols = slice(at_head * HD, (at_head + 1) * HD)
        for n, ref in enumerate(out_refs):
            ref[:, cols] = back_ref[at_head * copies, n * tok : (n + 1) * tok, :]
        if down_ref is not None:
            down_ref[:, cols] = back_ref[at_head * copies, 3 * tok :, :].astype(jnp.float32)


def in_vmem(body, outs, *operands):
    whole = pl.BlockSpec(memory_space=pltpu.VMEM)
    size = sum(x.size * x.dtype.itemsize for x in operands)
    size += sum(x.size * x.dtype.itemsize for x in outs)
    return pl.pallas_call(
        body,
        out_shape=outs,
        in_specs=[whole] * len(operands),
        out_specs=[whole] * len(outs),
        compiler_params=pltpu.CompilerParams(vmem_limit_bytes=16 * 1024 * 1024),
        cost_estimate=pl.CostEstimate(flops=0, bytes_accessed=size, transcendentals=0),
    )(*operands)


def staged_kernel(from_ref, to_ref, sems):
    count = sems.shape[0]
    size = from_ref.shape[0] // count
    copies = [
        pltpu.make_async_copy(
            from_ref.at[pl.ds(n * size, size), :], to_ref.at[pl.ds(n * size, size), :], sems.at[n]
        )
        for n in range(count)
    ]
    for copy in copies:
        copy.start()
    for copy in copies:
        copy.wait()


def staged(value, limit):
    return pl.pallas_call(
        staged_kernel,
        out_shape=shape_of(value.shape, value.dtype),
        in_specs=[pl.BlockSpec(memory_space=pltpu.HBM)],
        out_specs=pl.BlockSpec(memory_space=pltpu.VMEM),
        scratch_shapes=[pltpu.SemaphoreType.DMA((4,))],
        compiler_params=pltpu.CompilerParams(vmem_limit_bytes=limit * 1024 * 1024),
        cost_estimate=pl.CostEstimate(
            flops=0, bytes_accessed=2 * value.size * value.dtype.itemsize, transcendentals=0
        ),
    )(value)


def cotangent_kernel(chunks, plan_ref, *refs):
    pieces, (matrix_ref, up_ref, down_ref, own_ref, sent_ref) = refs[:-5], refs[-5:]
    tok, cols = pieces[0].shape
    feats, low_rank = down_ref.shape
    count = len(pieces)
    if chunks == 1:
        stacks = [(jnp.concatenate([p[...] for p in pieces], axis=0), pl.ds(0, cols))]
    else:
        stacks = [
            (p[...], pl.ds(pl.multiple_of(plan_ref[count + k], HD), cols))
            for k, p in enumerate(pieces)
        ]
    mine = [plan_ref[k] == 1 for k in range(count)]

    def store(here, terms):
        parts = [t[:, i : i + tok] for t in terms for i in range(0, t.shape[1], tok)]
        own = [jnp.where(m, p, 0.0) for m, p in zip(mine, parts)]
        sent = [jnp.where(m, 0.0, p) for m, p in zip(mine, parts)]
        own_ref[here, :] = functools.reduce(jnp.add, own)
        sent_ref[here, :] = functools.reduce(jnp.add, sent).astype(jnp.bfloat16)

    loras = [dot_nt(up_ref[:, at], rows) for rows, at in stacks]
    store(pl.ds(feats, low_rank), loras)
    for first in range(0, feats, TILE):
        here = pl.ds(first, TILE)
        terms = [
            dot_nt(matrix_ref[here, at], rows)
            + 2.0 * dot_nn(down_ref[here, :], lora.astype(jnp.bfloat16))
            for (rows, at), lora in zip(stacks, loras)
        ]
        store(here, terms)


def dout_kernel(copies, own_ref, taken_ref, mid_ref, message_ref):
    low_rank = mid_ref.shape[1]
    feats = own_ref.shape[0] - low_rank
    lora = own_ref[feats:, :] + taken_ref[feats:, :].astype(jnp.float32)
    for rank in range(message_ref.shape[0]):
        at = pl.ds((rank // copies) * HD, HD)
        part = own_ref[at, :] + taken_ref[at, :].astype(jnp.float32)
        message_ref[rank, 0:HD, :] = part.astype(jnp.bfloat16)
        message_ref[rank, HD : HD + low_rank, :] = lora.astype(jnp.bfloat16)
        message_ref[rank, HD + low_rank : HD + 2 * low_rank, :] = mid_ref[rank]


def on_device(
    sizes,
    head_query_rows,
    head_key_rows,
    head_value_rows,
    output_gradient,
    output_matrix,
    adapter_down_weight,
    adapter_up_weight,
):
    seqs, heads, subs = sizes
    tok, feats = head_query_rows.shape
    cols = output_gradient.shape[1]
    low_rank = adapter_up_weight.shape[0]
    local_heads = feats // HD
    block_rows = tok * subs
    ranks = GROUP // block_rows
    copies = ranks // local_heads
    shift_blocks = GROUP // 2 // block_rows

    seq = lax.axis_index("seq")
    head = lax.axis_index("head")
    sub = lax.axis_index("sub")
    shifted = head >= heads // 2
    rank = (seq + shift_blocks) % ranks
    my_head = rank // copies

    groups = []
    for at_head in range(heads):
        for first in range(0, seqs, ranks):
            members = [first + shift_blocks + i for i in range(ranks)]
            if at_head < heads // 2:
                members = [first + (m - first) % ranks for m in members]
            members = [m % seqs for m in members]
            groups.append([m * heads + at_head for m in members])
    turned = jnp.where(shifted, 0, shift_blocks)
    scalars = jnp.stack((sub, turned)).astype(jnp.int32)

    def exchange(parts):
        return lax.all_to_all(
            parts, ("seq", "head"), 0, 0, axis_index_groups=groups, tiled=True
        )

    def swap(value):
        if subs == 1:
            return value
        return lax.ppermute(value, "sub", [(0, 1), (1, 0)])

    sent = message_of(copies, ranks, head_query_rows, head_key_rows, head_value_rows)
    sent, output_gradient, output_matrix = lax.optimization_barrier(
        (sent, output_gradient, output_matrix)
    )
    own = exchange(sent)

    chunks = heads // subs
    pieces = []
    for k in range(heads):
        pairs = []
        for src_head in range(heads):
            for src_sub in range(subs):
                j = (src_head % chunks) * subs + src_sub
                dst = ((j + k) % heads) * subs + src_head // chunks
                pairs.append((src_head * subs + src_sub, dst))
        pieces.append(lax.ppermute(output_gradient, ("head", "sub"), pairs))

    up_half = lax.dynamic_slice_in_dim(adapter_up_weight, sub * chunks * cols, chunks * cols, 1)
    sources = [(head - k + heads) % heads for k in range(heads)]
    plan = [(j % subs == sub).astype(jnp.int32) for j in sources]
    plan += [(j // subs * cols).astype(jnp.int32) for j in sources]
    packed_own, packed_sent = call_kernel(
        functools.partial(cotangent_kernel, chunks),
        [
            shape_of((feats + low_rank, tok), jnp.float32),
            shape_of((feats + low_rank, tok), jnp.bfloat16),
        ],
        [],
        0,
        0,
        jnp.stack(plan),
        *pieces,
        staged(output_matrix, 55),
        up_half,
        adapter_down_weight,
        declared=1024,
        limit=16,
    )
    received = swap(packed_sent)
    own, _ = lax.optimization_barrier((own, packed_sent))
    other = swap(own[:, tok:])

    down_head = lax.dynamic_slice_in_dim(adapter_down_weight, my_head * HD, HD, 0)
    rows = ranks * tok
    pair_count = rows * (rows + TILE)
    attn_t, middle_rows, stats = call_kernel(
        functools.partial(forward_kernel, tok),
        [
            shape_of((HD, rows), jnp.bfloat16),
            shape_of((ranks, low_rank, tok), jnp.bfloat16),
            shape_of((8, rows), jnp.float32),
        ],
        [],
        4 * pair_count * HD,
        pair_count,
        scalars,
        own,
        other,
        down_head.T,
        limit=16,
    )

    first_copy = rank % copies == 0
    if copies > 1:
        middle_rows = jnp.where(first_copy, middle_rows, 0.0)
    (message,) = in_vmem(
        functools.partial(dout_kernel, copies),
        [shape_of((ranks, HD + 2 * low_rank, tok), jnp.bfloat16)],
        packed_own,
        received,
        middle_rows,
    )
    arrived = exchange(message)
    middle = jnp.sum(arrived[:, HD + low_rank :].astype(jnp.float32), axis=0)
    bit = 1
    while bit < heads:
        middle += lax.ppermute(middle, "head", [(i, i ^ bit) for i in range(heads)])
        bit *= 2
    up_part = 2.0 * dot_nn(middle.astype(jnp.bfloat16), output_gradient)

    dq, dk_own, dv_own, pair_other, down_part = call_kernel(
        functools.partial(backward_kernel, tok),
        [
            shape_of((ranks, tok, HD), jnp.bfloat16),
            shape_of((ranks, tok, HD), jnp.float32),
            shape_of((ranks, tok, HD), jnp.float32),
            shape_of((ranks, 2 * tok, HD), jnp.bfloat16),
            shape_of((low_rank, HD), jnp.float32),
        ],
        [pltpu.VMEM((rows, HD), jnp.float32)] * 4,
        10 * pair_count * HD,
        pair_count,
        scalars,
        own,
        other,
        arrived,
        attn_t,
        stats,
        limit=28,
    )
    pair_received = swap(pair_other).astype(jnp.float32)
    down_rows = jnp.where(first_copy, down_part + swap(down_part), 0.0)
    dk = (dk_own + pair_received[:, :tok]).astype(jnp.bfloat16)
    dv = (dv_own + pair_received[:, tok:]).astype(jnp.bfloat16)
    down_rows = jnp.broadcast_to(down_rows.astype(jnp.bfloat16), (ranks, low_rank, HD))
    back_message = jnp.concatenate([dq, dk, dv, down_rows], axis=1)
    back = exchange(back_message)
    outs = [shape_of((tok, feats), back.dtype)] * 3
    if seqs == ranks:
        outs.append(shape_of((low_rank, feats), jnp.float32))
    outs = list(in_vmem(functools.partial(unpack_kernel, copies), outs, back))
    if seqs > ranks:
        bits = [bit for bit in powers_below(seqs) if bit >= ranks]
        down_terms = back[::copies, 3 * tok :].astype(jnp.float32)
        down_terms = butterfly_sum(down_terms, "seq", bits, seqs)
        outs.append(down_terms.transpose(1, 0, 2).reshape(low_rank, feats))
    query_gradient, key_gradient, value_gradient, down_gradient = outs

    up_sum = butterfly_sum(up_part, "seq", powers_below(seqs), seqs)
    _, up_sum = lax.optimization_barrier((back, up_sum))
    up_gradient = butterfly_sum(up_sum, "sub", powers_below(subs), subs)
    return (query_gradient, key_gradient, value_gradient, down_gradient.T, up_gradient)


def solution(mesh):
    rows = P(("rep", "seq", "sub"), "head")
    sizes = (mesh.shape["seq"], mesh.shape["head"], mesh.shape["sub"])
    return jax.shard_map(
        functools.partial(on_device, sizes),
        mesh=mesh,
        in_specs=(rows, rows, rows, rows, P("head", "sub"), P("head", None), P()),
        out_specs=(rows, rows, rows, P(("rep", "head"), None), P("rep", "head")),
        check_vma=False,
    )
```

profile of v0, /device:TPU:0, one launch (start us, length us, event | category | flops | bytes accessed | tf_op | source)
XLA Modules:
  0.0 90.9 jit_solution(5801138389501407532)
XLA Ops:
  0.7 2.1 %shard_map.110 = bf16[8,384,128]{2,1,0:T(8,128)(2,1)} custom-call(bf16[128,1024]{1,0:T(8,128)(2,1)} %refs_0_.1, bf16[128,1024]{1,0:T(8,128)(2,1)} %refs_1_.1, bf16[128,1024]{1,0:T(8,128)(2,1)} %refs_2_.1), custom_call_target="tpu_custom_call" | custom-call | bytes 1572864 | tf_op jit(solution)/shard_map/pallas_call | solution.py:244
  2.8 7.9 %all-to-all-start = ((bf16[8,384,128]{2,1,0:T(8,128)(2,1)}), bf16[8,384,128]{2,1,0:T(8,128)(2,1)S(1)}, u32[]{:S(2)}, u32[]{:S(2)}) async-start(bf16[8,384,128]{2,1,0:T(8,128)(2,1)} %shard_map.110), calls=%async_computation | async-start | bytes 1572864 | tf_op jit(solution)/shard_map/all_to_all | solution.py:395
  10.7 0.7 collective-permute-start
  11.3 2.7 %collective-permute-start.1 = (bf16[128,2048]{1,0:T(8,128)(2,1)S(1)}, bf16[128,2048]{1,0:T(8,128)(2,1)S(1)}, u32[]{:S(2)}, u32[]{:S(2)}) collective-permute-start(bf16[128,2048]{1,0:T(8,128)(2,1)S(1)} %copy-done.2), channel_id=1, source_target_pairs={{0,2},{1,0},{2,3},{3,1},{4,6},{5,4},{6,7},{7,5},{8,10},{9,8},{10,1... | collective-permute-start | bytes 1572872 | tf_op jit(solution)/shard_map/ppermute | solution.py:419
  14.1 4.2 %shard_map.111.refs_2_ = bf16[1024,2048]{1,0:T(8,128)(2,1)} custom-call(bf16[1024,2048]{1,0:T(8,128)(2,1)} %from_ref), custom_call_target="tpu_custom_call" | custom-call | bytes 8388608 | tf_op jit(solution)/shard_map/pallas_call | solution.py:298
  18.5 7.2 %collective-permute-done.1.refs_1_ = bf16[128,2048]{1,0:T(8,128)(2,1)S(1)} collective-permute-done((bf16[128,2048]{1,0:T(8,128)(2,1)S(1)}, bf16[128,2048]{1,0:T(8,128)(2,1)S(1)}, u32[]{:S(2)}, u32[]{:S(2)}) %collective-permute-start.1) | collective-permute-done | bytes 524320 | tf_op jit(solution)/shard_map/ppermute | solution.py:419
  25.8 2.2 %copy-done.1 = bf16[1024,2048]{1,0:T(8,128)(2,1)S(1)} copy-done((bf16[1024,2048]{1,0:T(8,128)(2,1)S(1)}, bf16[1024,2048]{1,0:T(8,128)(2,1)}, u32[]{:S(2)}) %copy-start.1) | copy-done | bytes 4194328
  28.0 2.9 %shard_map.112 = (f32[1040,128]{1,0:T(8,128)S(1)}, bf16[1040,128]{1,0:T(8,128)(2,1)S(1)}) custom-call(s32[4]{0:T(128)S(1)} %pad_add_fusion.1.plan_ref, bf16[128,2048]{1,0:T(8,128)(2,1)S(1)} %collective-permute-done.refs_0_, bf16[128,2048]{1,0:T(8,128)(2,1)S(1)} %collective-permute-done.1.refs_1_, bf16[1024,2048]{1,0:T(8,128)(2,1)S(1)} %copy-done.1, ...), custom_call_target="tpu_custom_call" | custom-call | bytes 1024 | tf_op jit(solution)/shard_map/pallas_call | solution.py:185
  30.8 0.8 slice.12
  31.7 0.9 collective-permute-start.2
  32.6 0.7 dynamic-slice_bitcast_fusion.refs_1_
  33.3 1.4 %collective-permute-done.2.refs_0_ = bf16[8,256,128]{2,1,0:T(8,128)(2,1)S(1)} collective-permute-done((bf16[8,256,128]{2,1,0:T(8,128)(2,1)}, bf16[8,256,128]{2,1,0:T(8,128)(2,1)S(1)}, u32[]{:S(2)}, u32[]{:S(2)}) %collective-permute-start.2) | collective-permute-done | bytes 524320 | tf_op jit(solution)/shard_map/ppermute | solution.py:402
  34.7 3.8 %shard_map.113 = (bf16[128,1024]{1,0:T(8,128)(2,1)S(1)}, bf16[8,16,128]{2,1,0:T(8,128)(2,1)S(1)}, f32[8,1024]{1,0:T(8,128)S(1)}) custom-call(s32[2]{0:T(128)S(1)} %pad_add_fusion.scalar_ref, bf16[8,384,128]{2,1,0:T(8,128)(2,1)S(1)} %all-to-all-done.own_ref, bf16[8,256,128]{2,1,0:T(8,128)(2,1)S(1)} %collective-permute-done.2.refs_0_, ...), custom_call_target="tpu_custom_call" | custom-call | flops 671088640 | bytes 1642504 | tf_op jit(solution)/shard_map/pallas_call | solution.py:185
  38.5 14.3 %all_to_all.15.refs_1_ = bf16[8,160,128]{2,1,0:T(8,128)(2,1)S(1)} all-to-all(bf16[8,160,128]{2,1,0:T(8,128)(2,1)S(1)} %shard_map.114), channel_id=1, replica_groups={{16,20,24,28,0,4,8,12},{18,22,26,30,2,6,10,14},{17,21,25,29,1,5,9,13},{..., dimensions={0} | all-to-all | bytes 655360 | tf_op jit(solution)/shard_map/all_to_all | solution.py:395
  52.8 5.5 %shard_map.115 = (bf16[8,128,128]{2,1,0:T(8,128)(2,1)S(1)}, f32[8,128,128]{2,1,0:T(8,128)S(1)}, f32[8,128,128]{2,1,0:T(8,128)S(1)}, bf16[8,256,128]{2,1,0:T(8,128)(2,1)S(1)}, f32[16,128]{1,0:T(8,128)S(1)}) custom-call(s32[2]{0:T(128)S(1)} %pad_add_fusion.scalar_ref, bf16[8,384,128]{2,1,0:T(8,128)(2,1)S(1)} %all-to-all-done.own_ref, ...), custom_call_target="tpu_custom_call" | custom-call | flops 1677721600 | bytes 3776520 | tf_op jit(solution)/shard_map/pallas_call | solution.py:185
  58.4 1.5 %collective-permute-start.6 = (f32[16,128]{1,0:T(8,128)S(1)}, f32[16,128]{1,0:T(8,128)S(1)}, u32[]{:S(2)}, u32[]{:S(2)}) collective-permute-start(f32[16,128]{1,0:T(8,128)S(1)} %convert_reduce_fusion), channel_id=1, source_target_pairs={{0,2},{2,0},{1,3},{3,1},{4,6},{6,4},{5,7},{7,5},{8,10},{10,8},{9,1... | collective-permute-start | bytes 24584 | tf_op jit(solution)/shard_map/ppermute | solution.py:480
  60.1 2.0 %collective-permute-done.6 = f32[16,128]{1,0:T(8,128)S(1)} collective-permute-done((f32[16,128]{1,0:T(8,128)S(1)}, f32[16,128]{1,0:T(8,128)S(1)}, u32[]{:S(2)}, u32[]{:S(2)}) %collective-permute-start.6) | collective-permute-done | bytes 8224 | tf_op jit(solution)/shard_map/ppermute | solution.py:480
  62.3 0.9 collective-permute-start.7
  63.4 1.0 %pad_maximum_fusion = bf16[8,400,128]{2,1,0:T(8,128)(2,1)} fusion(bf16[8,16,128]{2,1,0:T(8,128)(2,1)S(1)} %broadcast_in_dim.5, bf16[8,128,128]{2,1,0:T(8,128)(2,1)S(1)} %get-tuple-element.44, bf16[8,128,128]{2,1,0:T(8,128)(2,1)S(1)} %get-tuple-element.43, bf16[8,128,128]{2,1,0:T(8,128)(2,1)S(1)} %get-tuple-element.33), kind=kLoop, calls=%fused_computation.2 | loop fusion | flops 3276800 | bytes 1638400 | tf_op jit(solution)/shard_map/concatenate | solution.py:509
  64.4 4.8 %all-to-all-start.2 = ((bf16[8,400,128]{2,1,0:T(8,128)(2,1)}), bf16[8,400,128]{2,1,0:T(8,128)(2,1)S(1)}, u32[]{:S(2)}, u32[]{:S(2)}) async-start(bf16[8,400,128]{2,1,0:T(8,128)(2,1)} %pad_maximum_fusion), calls=%async_computation.2 | async-start | bytes 1638400 | tf_op jit(solution)/shard_map/all_to_all | solution.py:395
  69.9 13.3 %collective-permute-done.8 = bf16[16,2048]{1,0:T(8,128)(2,1)S(1)} collective-permute-done((bf16[16,2048]{1,0:T(8,128)(2,1)S(1)}, bf16[16,2048]{1,0:T(8,128)(2,1)S(1)}, u32[]{:S(2)}, u32[]{:S(2)}) %collective-permute-start.8) | collective-permute-done | bytes 65568 | tf_op jit(solution)/shard_map/ppermute | solution.py:208
  83.2 2.5 %collective-permute-start.9 = (bf16[16,2048]{1,0:T(8,128)(2,1)S(1)}, bf16[16,2048]{1,0:T(8,128)(2,1)S(1)}, u32[]{:S(2)}, u32[]{:S(2)}) collective-permute-start(bf16[16,2048]{1,0:T(8,128)(2,1)S(1)} %add_convert_fusion), channel_id=1, source_target_pairs={{0,16},{4,20},{8,24},{12,28},{16,0},{20,4},{24,8},{28,12},{1,17},{... | collective-permute-start | bytes 196616 | tf_op jit(solution)/shard_map/ppermute | solution.py:208
  85.7 3.2 %collective-permute-done.9 = bf16[16,2048]{1,0:T(8,128)(2,1)S(1)} collective-permute-done((bf16[16,2048]{1,0:T(8,128)(2,1)S(1)}, bf16[16,2048]{1,0:T(8,128)(2,1)S(1)}, u32[]{:S(2)}, u32[]{:S(2)}) %collective-permute-start.9) | collective-permute-done | bytes 65568 | tf_op jit(solution)/shard_map/ppermute | solution.py:208
  89.0 1.1 %shard_map.116 = (bf16[128,1024]{1,0:T(8,128)(2,1)}, bf16[128,1024]{1,0:T(8,128)(2,1)}, bf16[128,1024]{1,0:T(8,128)(2,1)}, f32[16,1024]{1,0:T(8,128)}) custom-call(bf16[8,400,128]{2,1,0:T(8,128)(2,1)S(1)} %all-to-all-done.2.back_ref), custom_call_target="tpu_custom_call" | custom-call | bytes 1671168 | tf_op jit(solution)/shard_map/pallas_call | solution.py:272
  (35 shorter events, 2.6 us)
Async XLA Ops:
  0.6 17.9 %copy-start = (bf16[16,4096]{1,0:T(8,128)(2,1)S(1)}, bf16[16,4096]{1,0:T(8,128)(2,1)}, u32[]{:S(2)}) copy-start(bf16[16,4096]{1,0:T(8,128)(2,1)} %param.13) | copy-start | bytes 393220
  0.6 10.0 %copy-start.2 = (bf16[128,2048]{1,0:T(8,128)(2,1)S(1)}, bf16[128,2048]{1,0:T(8,128)(2,1)}, u32[]{:S(2)}) copy-start(bf16[128,2048]{1,0:T(8,128)(2,1)} %param.10) | copy-start | bytes 1572868
  2.8 28.0 %all-to-all-start = ((bf16[8,384,128]{2,1,0:T(8,128)(2,1)}), bf16[8,384,128]{2,1,0:T(8,128)(2,1)S(1)}, u32[]{:S(2)}, u32[]{:S(2)}) async-start(bf16[8,384,128]{2,1,0:T(8,128)(2,1)} %shard_map.110), calls=%async_computation | async-start | bytes 1572864 | tf_op jit(solution)/shard_map/all_to_all | solution.py:395
  10.7 7.9 %collective-permute-start = (bf16[128,2048]{1,0:T(8,128)(2,1)S(1)}, bf16[128,2048]{1,0:T(8,128)(2,1)S(1)}, u32[]{:S(2)}, u32[]{:S(2)}) collective-permute-start(bf16[128,2048]{1,0:T(8,128)(2,1)S(1)} %copy-done.2), channel_id=1, source_target_pairs={{0,0},{1,2},{2,1},{3,3},{4,4},{5,6},{6,5},{7,7},{8,8},{9,10},{10,9... | collective-permute-start | bytes 1572872 | tf_op jit(solution)/shard_map/ppermute | solution.py:419
  11.3 14.4 %collective-permute-start.1 = (bf16[128,2048]{1,0:T(8,128)(2,1)S(1)}, bf16[128,2048]{1,0:T(8,128)(2,1)S(1)}, u32[]{:S(2)}, u32[]{:S(2)}) collective-permute-start(bf16[128,2048]{1,0:T(8,128)(2,1)S(1)} %copy-done.2), channel_id=1, source_target_pairs={{0,2},{1,0},{2,3},{3,1},{4,6},{5,4},{6,7},{7,5},{8,10},{9,8},{10,1... | collective-permute-start | bytes 1572872 | tf_op jit(solution)/shard_map/ppermute | solution.py:419
  14.1 4.2 %copy-start.3 = (bf16[1024,16]{0,1:T(8,128)(2,1)S(1)}, bf16[1024,16]{0,1:T(8,128)(2,1)}, u32[]{:S(2)}) copy-start(bf16[1024,16]{0,1:T(8,128)(2,1)} %param.12) | copy-start | bytes 98308
  25.8 2.2 %copy-start.1 = (bf16[1024,2048]{1,0:T(8,128)(2,1)S(1)}, bf16[1024,2048]{1,0:T(8,128)(2,1)}, u32[]{:S(2)}) copy-start(bf16[1024,2048]{1,0:T(8,128)(2,1)} %shard_map.111.refs_2_) | copy-start | bytes 12582916
  31.7 3.0 %collective-permute-start.2 = (bf16[8,256,128]{2,1,0:T(8,128)(2,1)}, bf16[8,256,128]{2,1,0:T(8,128)(2,1)S(1)}, u32[]{:S(2)}, u32[]{:S(2)}) collective-permute-start(bf16[8,256,128]{2,1,0:T(8,128)(2,1)} %slice.12), channel_id=1, source_target_pairs={{0,1},{1,0},{2,3},{3,2},{4,5},{5,4},{6,7},{7,6},{8,9},{9,8},{10,11... | collective-permute-start | bytes 1572872 | tf_op jit(solution)/shard_map/ppermute | solution.py:402
  32.5 5.9 %collective-permute-start.3 = (bf16[1040,128]{1,0:T(8,128)(2,1)S(1)}, bf16[1040,128]{1,0:T(8,128)(2,1)S(1)}, u32[]{:S(2)}, u32[]{:S(2)}) collective-permute-start(bf16[1040,128]{1,0:T(8,128)(2,1)S(1)} %get-tuple-element.27), channel_id=1, source_target_pairs={{0,1},{1,0},{2,3},{3,2},{4,5},{5,4},{6,7},{7,6},{8,9},{9,8},{10,11... | collective-permute-start | bytes 798728 | tf_op jit(solution)/shard_map/ppermute | solution.py:402
  58.3 4.9 %collective-permute-start.4 = (bf16[8,256,128]{2,1,0:T(8,128)(2,1)S(1)}, bf16[8,256,128]{2,1,0:T(8,128)(2,1)S(1)}, u32[]{:S(2)}, u32[]{:S(2)}) collective-permute-start(bf16[8,256,128]{2,1,0:T(8,128)(2,1)S(1)} %get-tuple-element.35), channel_id=1, source_target_pairs={{0,1},{1,0},{2,3},{3,2},{4,5},{5,4},{6,7},{7,6},{8,9},{9,8},{10,11... | collective-permute-start | bytes 1572872 | tf_op jit(solution)/shard_map/ppermute | solution.py:402
  58.4 3.7 %collective-permute-start.6 = (f32[16,128]{1,0:T(8,128)S(1)}, f32[16,128]{1,0:T(8,128)S(1)}, u32[]{:S(2)}, u32[]{:S(2)}) collective-permute-start(f32[16,128]{1,0:T(8,128)S(1)} %convert_reduce_fusion), channel_id=1, source_target_pairs={{0,2},{2,0},{1,3},{3,1},{4,6},{6,4},{5,7},{7,5},{8,10},{10,8},{9,1... | collective-permute-start | bytes 24584 | tf_op jit(solution)/shard_map/ppermute | solution.py:480
  59.9 3.3 %collective-permute-start.5 = (f32[16,128]{1,0:T(8,128)S(1)}, f32[16,128]{1,0:T(8,128)S(1)}, u32[]{:S(2)}, u32[]{:S(2)}) collective-permute-start(f32[16,128]{1,0:T(8,128)S(1)} %get-tuple-element.37), channel_id=1, source_target_pairs={{0,1},{1,0},{2,3},{3,2},{4,5},{5,4},{6,7},{7,6},{8,9},{9,8},{10,11... | collective-permute-start | bytes 24584 | tf_op jit(solution)/shard_map/ppermute | solution.py:402
  62.3 6.9 %collective-permute-start.7 = (bf16[16,2048]{1,0:T(8,128)(2,1)S(1)}, bf16[16,2048]{1,0:T(8,128)(2,1)S(1)}, u32[]{:S(2)}, u32[]{:S(2)}) collective-permute-start(bf16[16,2048]{1,0:T(8,128)(2,1)S(1)} %fusion), channel_id=1, source_target_pairs={{0,4},{4,0},{8,12},{12,8},{16,20},{20,16},{24,28},{28,24},{1,5},{5... | collective-permute-start | bytes 196616 | tf_op jit(solution)/shard_map/ppermute | solution.py:208
  64.4 24.5 %all-to-all-start.2 = ((bf16[8,400,128]{2,1,0:T(8,128)(2,1)}), bf16[8,400,128]{2,1,0:T(8,128)(2,1)S(1)}, u32[]{:S(2)}, u32[]{:S(2)}) async-start(bf16[8,400,128]{2,1,0:T(8,128)(2,1)} %pad_maximum_fusion), calls=%async_computation.2 | async-start | bytes 1638400 | tf_op jit(solution)/shard_map/all_to_all | solution.py:395
  69.2 14.0 %collective-permute-start.8 = (bf16[16,2048]{1,0:T(8,128)(2,1)S(1)}, bf16[16,2048]{1,0:T(8,128)(2,1)S(1)}, u32[]{:S(2)}, u32[]{:S(2)}) collective-permute-start(bf16[16,2048]{1,0:T(8,128)(2,1)S(1)} %add_convert_fusion.1), channel_id=1, source_target_pairs={{0,8},{4,12},{8,0},{12,4},{16,24},{20,28},{24,16},{28,20},{1,9},{5... | collective-permute-start | bytes 196616 | tf_op jit(solution)/shard_map/ppermute | solution.py:208
  83.2 5.7 %collective-permute-start.9 = (bf16[16,2048]{1,0:T(8,128)(2,1)S(1)}, bf16[16,2048]{1,0:T(8,128)(2,1)S(1)}, u32[]{:S(2)}, u32[]{:S(2)}) collective-permute-start(bf16[16,2048]{1,0:T(8,128)(2,1)S(1)} %add_convert_fusion), channel_id=1, source_target_pairs={{0,16},{4,20},{8,24},{12,28},{16,0},{20,4},{24,8},{28,12},{1,17},{... | collective-permute-start | bytes 196616 | tf_op jit(solution)/shard_map/ppermute | solution.py:208
  88.9 1.3 %collective-permute-start.10 = (bf16[16,2048]{1,0:T(8,128)(2,1)S(1)}, bf16[16,2048]{1,0:T(8,128)(2,1)S(1)}, u32[]{:S(2)}, u32[]{:S(2)}) collective-permute-start(bf16[16,2048]{1,0:T(8,128)(2,1)S(1)} %convert_add_fusion.1), channel_id=1, source_target_pairs={{0,1},{1,0},{2,3},{3,2},{4,5},{5,4},{6,7},{7,6},{8,9},{9,8},{10,11... | collective-permute-start | bytes 196616 | tf_op jit(solution)/shard_map/ppermute | solution.py:208
where the time goes:
time: 91.3 us; the launch traced here: 90.9 us
  waiting for transfers between devices  27.3 us (30%)
  starting transfers between devices  22.8 us (25%)
  Pallas kernels  19.6 us (21%)
  blocking collectives  14.3 us (16%)
  local copies, waits for them, and re-layouts  3.91 us (4%)
  other arithmetic  2.04 us (2%)
    ppermute x4, waiting for transfers between devices, butterfly_sum(): taken = lax.ppermute(value, axis, pairs)  16.6 us
    all_to_all x1, blocking collectives, exchange(): lax.all_to_all(parts, ('seq', 'head'), 0, 0, axis_index_groups=groups, ti...  14.3 us
    all_to_all x2, starting transfers between devices, exchange(): lax.all_to_all(parts, ('seq', 'head'), 0, 0, axis_index_groups=groups, ti...  12.7 us
    pallas_call x3, Pallas kernels, call_kernel(): pl.pallas_call(body, out_shape=outs, in_specs=specs, out_specs=[pl.BlockS...  12.1 us
    ppermute x2, waiting for transfers between devices, on_device(): pieces.append(lax.ppermute(output_gradient, ('head', 'sub'), pairs))  7.24 us
    pallas_call x1, Pallas kernels, staged(): pl.pallas_call(staged_kernel, out_shape=shape_of(value.shape, value.dtype...  4.15 us
    ppermute x4, starting transfers between devices, butterfly_sum(): taken = lax.ppermute(value, axis, pairs)  4.09 us
    ppermute x2, starting transfers between devices, on_device(): pieces.append(lax.ppermute(output_gradient, ('head', 'sub'), pairs))  3.41 us
  transfers between devices with their start and end apart: 13, of which 6 were waited for; matrix products, arithmetic and copies ran while one was open for 3% of the time, Pallas kernels for 13%

commit v1 on v0

--- a/solution.py
+++ b/solution.py
@@ -26,31 +26,42 @@
     return jnp.dot(left, right, preferred_element_type=jnp.float32)
 
 
-def rows_of(ref, blocks, slot_of, first, count):
-    parts = [ref[slot_of(block), first : first + count, :] for block in blocks]
-    return jnp.concatenate(parts, axis=0)
+def rows_of(ref, run, first, count):
+    start, blocks = run
+    return ref[start : start + blocks, first : first + count, :].reshape(blocks * count, HD)
 
 
 def in_either_order(body, scalar_ref, blocks):
     for turn in (0, blocks // 2):
-        pl.when(scalar_ref[1] == turn)(
-            functools.partial(body, lambda block, turn=turn: (block + turn) % blocks)
-        )
-
-
-def scores_of(sub, keys_own, keys_other, queries, tok):
-    def tail_hidden(scores, visible):
-        head = scores.shape[0] - TILE
-        tail = jnp.where(visible, scores[head:], HIDDEN)
-        return tail if head == 0 else jnp.concatenate((scores[:head], tail), axis=0)
-
+        pl.when(scalar_ref[1] == turn)(functools.partial(body, turn))
+
+
+def runs_of(turn, blocks, upto):
+    whole = min(upto, blocks - turn)
+    return [(turn, whole)] + ([(0, upto - whole)] if upto > whole else [])
+
+
+def scores_of(queries, sides, runs, masks, tok):
+    scores = []
+    for (ref, first), visible in zip(sides, masks):
+        for n, run in enumerate(runs):
+            part = dot_nt(rows_of(ref, run, first, tok), queries)
+            if n == len(runs) - 1:
+                head = part.shape[0] - TILE
+                tail = jnp.where(visible, part[head:], HIDDEN)
+                part = tail if head == 0 else jnp.concatenate((part[:head], tail), axis=0)
+            scores.append(part)
+    return scores
+
+
+def masks_of(sub, tok):
     key_at = lax.broadcasted_iota(jnp.int32, (TILE, TILE), 0)
     query_at = lax.broadcasted_iota(jnp.int32, (TILE, TILE), 1)
-    own = tail_hidden(dot_nt(keys_own, queries), key_at <= query_at)
-    other = tail_hidden(
-        dot_nt(keys_other, queries), key_at // tok < query_at // tok + sub
-    )
-    return own, other
+    return key_at <= query_at, key_at // tok < query_at // tok + sub
+
+
+def summed(terms):
+    return functools.reduce(jnp.add, terms)
 
 
 def forward_kernel(tok, scalar_ref, own_ref, *refs):
@@ -59,38 +70,39 @@
 
 
 def forward_body(
-    tok, scalar_ref, own_ref, other_ref, down_t_ref, attn_ref, mid_ref, stat_ref, slot_of
+    tok, scalar_ref, own_ref, other_ref, down_t_ref, attn_ref, mid_ref, stat_ref, turn
 ):
     blocks = own_ref.shape[0]
     step = TILE // tok
-    sub = scalar_ref[0]
-    values_own_t = rows_of(own_ref, range(blocks), slot_of, 2 * tok, tok).T
-    values_other_t = rows_of(other_ref, range(blocks), slot_of, tok, tok).T
+    masks = masks_of(scalar_ref[0], tok)
+    sides = ((own_ref, tok), (other_ref, 0))
+    everything = (0, blocks)
+    values_t = [rows_of(ref, everything, first + tok, tok).T for ref, first in sides]
     for tile in range(blocks // step):
-        here = range(tile * step, (tile + 1) * step)
-        width = (tile + 1) * TILE
         at = tile * TILE
-        upto = range((tile + 1) * step)
-        queries = rows_of(own_ref, here, slot_of, 0, tok)
-        keys_own = rows_of(own_ref, upto, slot_of, tok, tok)
-        keys_other = rows_of(other_ref, upto, slot_of, 0, tok)
-        own, other = scores_of(sub, keys_own, keys_other, queries, tok)
-        highest = jnp.maximum(
-            jnp.max(own, axis=0, keepdims=True), jnp.max(other, axis=0, keepdims=True)
-        )
-        own = jnp.exp2((own - highest) * LOG2_SCALE)
-        other = jnp.exp2((other - highest) * LOG2_SCALE)
-        inverse = 1.0 / (
-            jnp.sum(own, axis=0, keepdims=True) + jnp.sum(other, axis=0, keepdims=True)
-        )
-        attn = dot_nn(values_own_t[:, :width], own.astype(jnp.bfloat16)) + dot_nn(
-            values_other_t[:, :width], other.astype(jnp.bfloat16)
+        start = (tile * step + turn) % blocks
+        runs = runs_of(turn, blocks, (tile + 1) * step)
+        queries = rows_of(own_ref, (start, step), 0, tok)
+        scores = scores_of(queries, sides, runs, masks, tok)
+        tops = [jnp.max(part, axis=0, keepdims=True) for part in scores]
+        highest = functools.reduce(jnp.maximum, tops)
+        powers = [jnp.exp2((part - highest) * LOG2_SCALE) for part in scores]
+        inverse = 1.0 / summed([jnp.sum(part, axis=0, keepdims=True) for part in powers])
+        places = [(n, run) for n in range(2) for run in runs]
+        attn = summed(
+            [
+                dot_nn(
+                    values_t[n][:, first * tok : (first + count) * tok],
+                    part.astype(jnp.bfloat16),
+                )
+                for (n, (first, count)), part in zip(places, powers)
+            ]
         )
         attn = (attn * inverse).astype(jnp.bfloat16)
         attn_ref[:, at : at + TILE] = attn
         mid = dot_nn(down_t_ref[...], attn)
-        for i, block in enumerate(here):
-            mid_ref[slot_of(block)] = mid[:, i * tok : (i + 1) * tok].astype(jnp.bfloat16)
+        for i in range(step):
+            mid_ref[start + i] = mid[:, i * tok : (i + 1) * tok].astype(jnp.bfloat16)
         stat_ref[0:1, at : at + TILE] = highest
         stat_ref[1:2, at : at + TILE] = inverse
 
@@ -117,67 +129,69 @@
     dv_own,
     dk_other,
     dv_other,
-    slot_of,
+    turn,
 ):
     blocks = own_ref.shape[0]
     step = TILE // tok
-    sub = scalar_ref[0]
     low_rank = down_grad_ref.shape[0]
-    keys_own_t = rows_of(own_ref, range(blocks), slot_of, tok, tok).T
-    keys_other_t = rows_of(other_ref, range(blocks), slot_of, 0, tok).T
+    masks = masks_of(scalar_ref[0], tok)
+    sides = ((own_ref, tok), (other_ref, 0))
+    everything = (0, blocks)
+    keys_t = [rows_of(ref, everything, first, tok).T for ref, first in sides]
+    dk, dv = (dk_own, dk_other), (dv_own, dv_other)
     tiles = blocks // step
     down_total = jnp.zeros((low_rank, HD), jnp.float32)
     for tile in reversed(range(tiles)):
-        here = range(tile * step, (tile + 1) * step)
-        width = (tile + 1) * TILE
         at = tile * TILE
-        queries = rows_of(own_ref, here, slot_of, 0, tok)
-        douts_t = jnp.concatenate([dout_ref[slot_of(b), 0:HD, :] for b in here], axis=1)
+        start = (tile * step + turn) % blocks
+        runs = runs_of(turn, blocks, (tile + 1) * step)
+        queries = rows_of(own_ref, (start, step), 0, tok)
+        douts_t = jnp.concatenate([dout_ref[start + i, 0:HD, :] for i in range(step)], axis=1)
         highest = stat_ref[0:1, at : at + TILE]
         inverse = stat_ref[1:2, at : at + TILE]
-        upto = range((tile + 1) * step)
-        keys_own = rows_of(own_ref, upto, slot_of, tok, tok)
-        keys_other = rows_of(other_ref, upto, slot_of, 0, tok)
-        own, other = scores_of(sub, keys_own, keys_other, queries, tok)
-        own = jnp.exp2((own - highest) * LOG2_SCALE) * inverse
-        other = jnp.exp2((other - highest) * LOG2_SCALE) * inverse
-        dprob_own = dot_nn(rows_of(own_ref, upto, slot_of, 2 * tok, tok), douts_t)
-        dprob_other = dot_nn(rows_of(other_ref, upto, slot_of, tok, tok), douts_t)
-        delta = jnp.sum(own * dprob_own, axis=0, keepdims=True) + jnp.sum(
-            other * dprob_other, axis=0, keepdims=True
+        scores = scores_of(queries, sides, runs, masks, tok)
+        places = [(n, run) for n in range(2) for run in runs]
+        probs = [jnp.exp2((part - highest) * LOG2_SCALE) * inverse for part in scores]
+        dprobs = [
+            dot_nn(rows_of(sides[n][0], run, sides[n][1] + tok, tok), douts_t)
+            for n, run in places
+        ]
+        delta = summed(
+            [jnp.sum(p * d, axis=0, keepdims=True) for p, d in zip(probs, dprobs)]
         )
-        ds_own = (own * (dprob_own - delta)).astype(jnp.bfloat16)
-        ds_other = (other * (dprob_other - delta)).astype(jnp.bfloat16)
-        dq = dot_nn(keys_own_t[:, :width], ds_own) + dot_nn(keys_other_t[:, :width], ds_other)
+        dscores = [(p * (d - delta)).astype(jnp.bfloat16) for p, d in zip(probs, dprobs)]
+        dq = summed(
+            [
+                dot_nn(keys_t[n][:, first * tok : (first + count) * tok], part)
+                for (n, (first, count)), part in zip(places, dscores)
+            ]
+        )
         dq = (dq * SCALE).T.astype(jnp.bfloat16)
-        terms = (
-            (dk_own, dot_nn(ds_own, queries)),
-            (dk_other, dot_nn(ds_other, queries)),
-            (dv_own, dot_nt(own.astype(jnp.bfloat16), douts_t)),
-            (dv_other, dot_nt(other.astype(jnp.bfloat16), douts_t)),
-        )
-        for total, term in terms:
+        for (n, (first, count)), prob, dscore in zip(places, probs, dscores):
+            rows = pl.ds(first * tok, count * tok)
+            dk_term = dot_nn(dscore, queries)
+            dv_term = dot_nt(prob.astype(jnp.bfloat16), douts_t)
             if tile == tiles - 1:
-                total[...] = term
+                dk[n][rows, :] = dk_term
+                dv[n][rows, :] = dv_term
             else:
-                total[0:width] += term
-        for i, block in enumerate(here):
-            slot = slot_of(block)
+                dk[n][rows, :] += dk_term
+                dv[n][rows, :] += dv_term
+        for i in range(step):
+            slot = start + i
             dq_ref[slot] = dq[i * tok : (i + 1) * tok]
             lora = dout_ref[slot, HD : HD + low_rank, :]
             attn = attn_ref[:, at + i * tok : at + (i + 1) * tok]
             down_total += dot_nt(lora, attn)
-    for block in range(blocks):
-        rows = pl.ds(block * tok, tok)
-        slot = slot_of(block)
-        dk_own_ref[slot] = dk_own[rows, :] * SCALE
-        dv_own_ref[slot] = dv_own[rows, :]
-        pair_other_ref[slot, 0:tok, :] = (dk_other[rows, :] * SCALE).astype(jnp.bfloat16)
-        pair_other_ref[slot, tok : 2 * tok, :] = dv_other[rows, :].astype(jnp.bfloat16)
+    shape = (blocks, tok, HD)
+    dk_own_ref[...] = (dk_own[...] * SCALE).reshape(shape)
+    dv_own_ref[...] = dv_own[...].reshape(shape)
+    pair_other_ref[:, 0:tok, :] = (dk_other[...] * SCALE).astype(jnp.bfloat16).reshape(shape)
+    pair_other_ref[:, tok : 2 * tok, :] = dv_other[...].astype(jnp.bfloat16).reshape(shape)
     down_grad_ref[...] = 2.0 * down_total
 
 
-def call_kernel(body, outs, scratch, flops, exps, *operands, declared=None, limit=48):
+def call_kernel(body, outs, scratch, flops, exps, *operands, limit=48):
     in_bytes = sum(x.size * x.dtype.itemsize for x in operands)
     out_bytes = sum(x.size * x.dtype.itemsize for x in outs)
     specs = [pl.BlockSpec(memory_space=pltpu.SMEM)]
@@ -191,7 +205,7 @@
         compiler_params=pltpu.CompilerParams(vmem_limit_bytes=limit * 1024 * 1024),
         cost_estimate=pl.CostEstimate(
             flops=flops,
-            bytes_accessed=declared or in_bytes + out_bytes,
+            bytes_accessed=in_bytes + out_bytes,
             transcendentals=exps,
         ),
     )(*operands)
@@ -279,68 +293,6 @@
     )(*operands)
 
 
-def staged_kernel(from_ref, to_ref, sems):
-    count = sems.shape[0]
-    size = from_ref.shape[0] // count
-    copies = [
-        pltpu.make_async_copy(
-            from_ref.at[pl.ds(n * size, size), :], to_ref.at[pl.ds(n * size, size), :], sems.at[n]
-        )
-        for n in range(count)
-    ]
-    for copy in copies:
-        copy.start()
-    for copy in copies:
-        copy.wait()
-
-
-def staged(value, limit):
-    return pl.pallas_call(
-        staged_kernel,
-        out_shape=shape_of(value.shape, value.dtype),
-        in_specs=[pl.BlockSpec(memory_space=pltpu.HBM)],
-        out_specs=pl.BlockSpec(memory_space=pltpu.VMEM),
-        scratch_shapes=[pltpu.SemaphoreType.DMA((4,))],
-        compiler_params=pltpu.CompilerParams(vmem_limit_bytes=limit * 1024 * 1024),
-        cost_estimate=pl.CostEstimate(
-            flops=0, bytes_accessed=2 * value.size * value.dtype.itemsize, transcendentals=0
-        ),
-    )(value)
-
-
-def cotangent_kernel(chunks, plan_ref, *refs):
-    pieces, (matrix_ref, up_ref, down_ref, own_ref, sent_ref) = refs[:-5], refs[-5:]
-    tok, cols = pieces[0].shape
-    feats, low_rank = down_ref.shape
-    count = len(pieces)
-    if chunks == 1:
-        stacks = [(jnp.concatenate([p[...] for p in pieces], axis=0), pl.ds(0, cols))]
-    else:
-        stacks = [
-            (p[...], pl.ds(pl.multiple_of(plan_ref[count + k], HD), cols))
-            for k, p in enumerate(pieces)
-        ]
-    mine = [plan_ref[k] == 1 for k in range(count)]
-
-    def store(here, terms):
-        parts = [t[:, i : i + tok] for t in terms for i in range(0, t.shape[1], tok)]
-        own = [jnp.where(m, p, 0.0) for m, p in zip(mine, parts)]
-        sent = [jnp.where(m, 0.0, p) for m, p in zip(mine, parts)]
-        own_ref[here, :] = functools.reduce(jnp.add, own)
-        sent_ref[here, :] = functools.reduce(jnp.add, sent).astype(jnp.bfloat16)
-
-    loras = [dot_nt(up_ref[:, at], rows) for rows, at in stacks]
-    store(pl.ds(feats, low_rank), loras)
-    for first in range(0, feats, TILE):
-        here = pl.ds(first, TILE)
-        terms = [
-            dot_nt(matrix_ref[here, at], rows)
-            + 2.0 * dot_nn(down_ref[here, :], lora.astype(jnp.bfloat16))
-            for (rows, at), lora in zip(stacks, loras)
-        ]
-        store(here, terms)
-
-
 def dout_kernel(copies, own_ref, taken_ref, mid_ref, message_ref):
     low_rank = mid_ref.shape[1]
     feats = own_ref.shape[0] - low_rank
@@ -402,9 +354,7 @@
         return lax.ppermute(value, "sub", [(0, 1), (1, 0)])
 
     sent = message_of(copies, ranks, head_query_rows, head_key_rows, head_value_rows)
-    sent, output_gradient, output_matrix = lax.optimization_barrier(
-        (sent, output_gradient, output_matrix)
-    )
+    sent, output_gradient = lax.optimization_barrier((sent, output_gradient))
     own = exchange(sent)
 
     chunks = heads // subs
@@ -420,27 +370,26 @@
 
     up_half = lax.dynamic_slice_in_dim(adapter_up_weight, sub * chunks * cols, chunks * cols, 1)
     sources = [(head - k + heads) % heads for k in range(heads)]
-    plan = [(j % subs == sub).astype(jnp.int32) for j in sources]
-    plan += [(j // subs * cols).astype(jnp.int32) for j in sources]
-    packed_own, packed_sent = call_kernel(
-        functools.partial(cotangent_kernel, chunks),
-        [
-            shape_of((feats + low_rank, tok), jnp.float32),
-            shape_of((feats + low_rank, tok), jnp.bfloat16),
-        ],
-        [],
-        0,
-        0,
-        jnp.stack(plan),
-        *pieces,
-        staged(output_matrix, 55),
-        up_half,
-        adapter_down_weight,
-        declared=1024,
-        limit=16,
-    )
-    received = swap(packed_sent)
-    own, _ = lax.optimization_barrier((own, packed_sent))
+    _, pieces = lax.optimization_barrier((own, pieces))
+
+    def terms_of(rows, at):
+        matrix, up = output_matrix, up_half
+        if chunks > 1:
+            matrix = lax.dynamic_slice_in_dim(matrix, at, cols, 1)
+            up = lax.dynamic_slice_in_dim(up, at, cols, 1)
+        lora = dot_nt(up, rows)
+        grad = dot_nt(matrix, rows)
+        grad += 2.0 * dot_nn(adapter_down_weight, lora.astype(jnp.bfloat16))
+        return jnp.concatenate((grad, lora), axis=0)
+
+    if chunks == 1:
+        terms = jnp.split(terms_of(jnp.concatenate(pieces, axis=0), 0), heads, axis=1)
+    else:
+        terms = [terms_of(p, j // subs * cols) for p, j in zip(pieces, sources)]
+    mine = [j % subs == sub for j in sources]
+    packed_own = summed([jnp.where(m, t, 0.0) for m, t in zip(mine, terms)])
+    packed_sent = summed([jnp.where(m, 0.0, t) for m, t in zip(mine, terms)])
+    received = swap(packed_sent.astype(jnp.bfloat16))
     other = swap(own[:, tok:])
 
     down_head = lax.dynamic_slice_in_dim(adapter_down_weight, my_head * HD, HD, 0)

time: 91.3 us -> 88.9 us (0.974)
  Pallas kernels: 19.6 us -> 12.8 us
  waiting for transfers between devices: 27.3 us -> 32.8 us
  local copies, waits for them, and re-layouts: 3.91 us -> 1.42 us
  matrix products: 0.19 us -> 2.19 us
    ppermute x2, waiting for transfers between devices: 7.24 us -> 11.7 us  [on_device(): pieces.append(lax.ppermute(output_gradient, ('head', 'sub'), pairs))]
    pallas_call x1 -> x0, Pallas kernels: 4.15 us -> none  [staged(): pl.pallas_call(staged_kernel, out_shape=shape_of(value.shape, value.dtype...]
    pallas_call x3 -> x2, Pallas kernels: 12.1 us -> 9.45 us  [call_kernel(): pl.pallas_call(body, out_shape=outs, in_specs=specs, out_specs=[pl.BlockS...]
    all_to_all x2, waiting for transfers between devices: 0.01 us -> 2.35 us  [exchange(): lax.all_to_all(parts, ('seq', 'head'), 0, 0, axis_index_groups=groups, ti...]
    dot_general x0 -> x2, matrix products: none -> 1.66 us  [dot_nt(): lax.dot_general(left, right, (((1,), (1,)), ((), ())), preferred_element_...]
    ppermute x4, waiting for transfers between devices: 1.37 us -> 0.01 us  [swap(): return lax.ppermute(value, 'sub', [(0, 1), (1, 0)])]
    unnamed x9, local copies, waits for them, and re-layouts: 2.37 us -> 1.34 us
  transfers between devices with their start and end apart: 13 -> 13, of which waited for: 6 -> 6; matrix products, arithmetic and copies ran while one was open for 3% -> 4% of each run, Pallas kernels for 13% -> 6%
where the time goes in v1:
time: 88.9 us; the launch traced here: 88.5 us
  waiting for transfers between devices  32.8 us (37%)
  starting transfers between devices  22 us (25%)
  blocking collectives  14.4 us (16%)
  Pallas kernels  12.8 us (14%)
  matrix products  2.19 us (2%)
  other arithmetic  2.09 us (2%)
  local copies, waits for them, and re-layouts  1.42 us (2%)
    ppermute x4, waiting for transfers between devices, butterfly_sum(): taken = lax.ppermute(value, axis, pairs)  16.6 us
    all_to_all x1, blocking collectives, exchange(): lax.all_to_all(parts, ('seq', 'head'), 0, 0, axis_index_groups=groups, ti...  14.4 us
    all_to_all x2, starting transfers between devices, exchange(): lax.all_to_all(parts, ('seq', 'head'), 0, 0, axis_index_groups=groups, ti...  12.7 us
    ppermute x2, waiting for transfers between devices, on_device(): pieces.append(lax.ppermute(output_gradient, ('head', 'sub'), pairs))  11.7 us
    pallas_call x2, Pallas kernels, call_kernel(): pl.pallas_call(body, out_shape=outs, in_specs=specs, out_specs=[pl.BlockS...  9.45 us
    ppermute x4, starting transfers between devices, butterfly_sum(): taken = lax.ppermute(value, axis, pairs)  4.1 us
    ppermute x2, starting transfers between devices, on_device(): pieces.append(lax.ppermute(output_gradient, ('head', 'sub'), pairs))  3.41 us
    all_to_all x2, waiting for transfers between devices, exchange(): lax.all_to_all(parts, ('seq', 'head'), 0, 0, axis_index_groups=groups, ti...  2.35 us
  transfers between devices with their start and end apart: 13, of which 6 were waited for; matrix products, arithmetic and copies ran while one was open for 4% of the time, Pallas kernels for 6%

profile of v1, /device:TPU:0, one launch (start us, length us, event | category | flops | bytes accessed | tf_op | source)
XLA Modules:
  0.0 88.5 jit_solution(12086348035074020375)
XLA Ops:
  0.7 2.1 %shard_map.110 = bf16[8,384,128]{2,1,0:T(8,128)(2,1)} custom-call(bf16[128,1024]{1,0:T(8,128)(2,1)} %refs_0_.1, bf16[128,1024]{1,0:T(8,128)(2,1)} %refs_1_.1, bf16[128,1024]{1,0:T(8,128)(2,1)} %refs_2_.1), custom_call_target="tpu_custom_call" | custom-call | bytes 1572864 | tf_op jit(solution)/shard_map/pallas_call | solution.py:258
  2.8 7.9 %all-to-all-start = ((bf16[8,384,128]{2,1,0:T(8,128)(2,1)}), bf16[8,384,128]{2,1,0:T(8,128)(2,1)S(1)}, u32[]{:S(2)}, u32[]{:S(2)}) async-start(bf16[8,384,128]{2,1,0:T(8,128)(2,1)} %shard_map.110), calls=%async_computation | async-start | bytes 1572864 | tf_op jit(solution)/shard_map/all_to_all | solution.py:347
  10.7 0.7 collective-permute-start.1
  11.3 2.7 %collective-permute-start.2 = (bf16[128,2048]{1,0:T(8,128)(2,1)S(1)}, bf16[128,2048]{1,0:T(8,128)(2,1)S(1)}, u32[]{:S(2)}, u32[]{:S(2)}) collective-permute-start(bf16[128,2048]{1,0:T(8,128)(2,1)S(1)} %copy-done.1), channel_id=1, source_target_pairs={{0,2},{1,0},{2,3},{3,1},{4,6},{5,4},{6,7},{7,5},{8,10},{9,8},{10,1... | collective-permute-start | bytes 1572872 | tf_op jit(solution)/shard_map/ppermute | solution.py:369
  14.1 11.7 %collective-permute-done.2 = bf16[128,2048]{1,0:T(8,128)(2,1)S(1)} collective-permute-done((bf16[128,2048]{1,0:T(8,128)(2,1)S(1)}, bf16[128,2048]{1,0:T(8,128)(2,1)S(1)}, u32[]{:S(2)}, u32[]{:S(2)}) %collective-permute-start.2) | collective-permute-done | bytes 524320 | tf_op jit(solution)/shard_map/ppermute | solution.py:369
  25.8 2.3 %all-to-all-done.own_ref = bf16[8,384,128]{2,1,0:T(8,128)(2,1)S(1)} async-done(((bf16[8,384,128]{2,1,0:T(8,128)(2,1)}), bf16[8,384,128]{2,1,0:T(8,128)(2,1)S(1)}, u32[]{:S(2)}, u32[]{:S(2)}) %all-to-all-start) | async-done | bytes 786464 | tf_op jit(solution)/shard_map/all_to_all | solution.py:347
  28.4 0.4 fusion.5
  28.9 0.3 convolution_multiply_fusion.1
  29.3 1.1 %copy-done.3 = bf16[1024,2048]{1,0:T(8,128)(2,1)S(1)} copy-done((bf16[1024,2048]{1,0:T(8,128)(2,1)S(1)}, bf16[1024,2048]{1,0:T(8,128)(2,1)}, u32[]{:S(2)}) %copy-start.3) | copy-done | bytes 4194328
  30.4 1.3 %fusion.1 = f32[1024,256]{1,0:T(8,128)S(1)} fusion(f32[256,1024]{0,1:T(8,128)S(1)} %convolution_multiply_fusion.1, bf16[256,2048]{1,0:T(8,128)(2,1)S(1)} %constant_dynamic-update-slice_fusion, bf16[1024,2048]{1,0:T(8,128)(2,1)S(1)} %copy-done.3), kind=kOutput, calls=%fused_computation.4 | convolution fusion | flops 1074003968 | bytes 7340032 | tf_op jit(solution)/shard_map/dot_general | solution.py:20
  32.0 4.1 %shard_map.111 = (bf16[128,1024]{1,0:T(8,128)(2,1)S(1)}, bf16[8,16,128]{2,1,0:T(8,128)(2,1)S(1)}, f32[8,1024]{1,0:T(8,128)S(1)}) custom-call(s32[2]{0:T(128)S(1)} %pad_add_fusion.scalar_ref, bf16[8,384,128]{2,1,0:T(8,128)(2,1)S(1)} %all-to-all-done.own_ref, bf16[8,256,128]{2,1,0:T(8,128)(2,1)S(1)} %collective-permute-done.refs_0_, ...), custom_call_target="tpu_custom_call" | custom-call | flops 671088640 | bytes 1642504 | tf_op jit(solution)/shard_map/pallas_call | solution.py:199
  36.1 14.4 %all_to_all.15.refs_1_ = bf16[8,160,128]{2,1,0:T(8,128)(2,1)S(1)} all-to-all(bf16[8,160,128]{2,1,0:T(8,128)(2,1)S(1)} %shard_map.112), channel_id=1, replica_groups={{16,20,24,28,0,4,8,12},{18,22,26,30,2,6,10,14},{17,21,25,29,1,5,9,13},{..., dimensions={0} | all-to-all | bytes 655360 | tf_op jit(solution)/shard_map/all_to_all | solution.py:347
  50.5 5.3 %shard_map.113 = (bf16[8,128,128]{2,1,0:T(8,128)(2,1)S(1)}, f32[8,128,128]{2,1,0:T(8,128)S(1)}, f32[8,128,128]{2,1,0:T(8,128)S(1)}, bf16[8,256,128]{2,1,0:T(8,128)(2,1)S(1)}, f32[16,128]{1,0:T(8,128)S(1)}) custom-call(s32[2]{0:T(128)S(1)} %pad_add_fusion.scalar_ref, bf16[8,384,128]{2,1,0:T(8,128)(2,1)S(1)} %all-to-all-done.own_ref, ...), custom_call_target="tpu_custom_call" | custom-call | flops 1677721600 | bytes 3776520 | tf_op jit(solution)/shard_map/pallas_call | solution.py:199
  56.0 1.4 %collective-permute-start.6 = (f32[16,128]{1,0:T(8,128)S(1)}, f32[16,128]{1,0:T(8,128)S(1)}, u32[]{:S(2)}, u32[]{:S(2)}) collective-permute-start(f32[16,128]{1,0:T(8,128)S(1)} %convert_reduce_fusion), channel_id=1, source_target_pairs={{0,2},{2,0},{1,3},{3,1},{4,6},{6,4},{5,7},{7,5},{8,10},{10,8},{9,1... | collective-permute-start | bytes 24584 | tf_op jit(solution)/shard_map/ppermute | solution.py:429
  57.6 2.1 %collective-permute-done.6 = f32[16,128]{1,0:T(8,128)S(1)} collective-permute-done((f32[16,128]{1,0:T(8,128)S(1)}, f32[16,128]{1,0:T(8,128)S(1)}, u32[]{:S(2)}, u32[]{:S(2)}) %collective-permute-start.6) | collective-permute-done | bytes 8224 | tf_op jit(solution)/shard_map/ppermute | solution.py:429
  59.9 0.9 %collective-permute-start.7 = (bf16[16,2048]{1,0:T(8,128)(2,1)S(1)}, bf16[16,2048]{1,0:T(8,128)(2,1)S(1)}, u32[]{:S(2)}, u32[]{:S(2)}) collective-permute-start(bf16[16,2048]{1,0:T(8,128)(2,1)S(1)} %fusion), channel_id=1, source_target_pairs={{0,4},{4,0},{8,12},{12,8},{16,20},{20,16},{24,28},{28,24},{1,5},{5... | collective-permute-start | bytes 196616 | tf_op jit(solution)/shard_map/ppermute | solution.py:222
  61.0 1.0 %pad_maximum_fusion = bf16[8,400,128]{2,1,0:T(8,128)(2,1)} fusion(bf16[8,16,128]{2,1,0:T(8,128)(2,1)S(1)} %broadcast_in_dim.14, bf16[8,128,128]{2,1,0:T(8,128)(2,1)S(1)} %get-tuple-element.42, bf16[8,128,128]{2,1,0:T(8,128)(2,1)S(1)} %get-tuple-element.41, bf16[8,128,128]{2,1,0:T(8,128)(2,1)S(1)} %get-tuple-element.29), kind=kLoop, calls=%fused_computation.7 | loop fusion | flops 3276800 | bytes 1638400 | tf_op jit(solution)/shard_map/concatenate | solution.py:458
  62.0 4.8 %all-to-all-start.2 = ((bf16[8,400,128]{2,1,0:T(8,128)(2,1)}), bf16[8,400,128]{2,1,0:T(8,128)(2,1)S(1)}, u32[]{:S(2)}, u32[]{:S(2)}) async-start(bf16[8,400,128]{2,1,0:T(8,128)(2,1)} %pad_maximum_fusion), calls=%async_computation.2 | async-start | bytes 1638400 | tf_op jit(solution)/shard_map/all_to_all | solution.py:347
  66.8 0.6 collective-permute-start.8
  67.5 13.3 %collective-permute-done.8 = bf16[16,2048]{1,0:T(8,128)(2,1)S(1)} collective-permute-done((bf16[16,2048]{1,0:T(8,128)(2,1)S(1)}, bf16[16,2048]{1,0:T(8,128)(2,1)S(1)}, u32[]{:S(2)}, u32[]{:S(2)}) %collective-permute-start.8) | collective-permute-done | bytes 65568 | tf_op jit(solution)/shard_map/ppermute | solution.py:222
  80.8 2.5 %collective-permute-start.9 = (bf16[16,2048]{1,0:T(8,128)(2,1)S(1)}, bf16[16,2048]{1,0:T(8,128)(2,1)S(1)}, u32[]{:S(2)}, u32[]{:S(2)}) collective-permute-start(bf16[16,2048]{1,0:T(8,128)(2,1)S(1)} %add_convert_fusion.1), channel_id=1, source_target_pairs={{0,16},{4,20},{8,24},{12,28},{16,0},{20,4},{24,8},{28,12},{1,17},{... | collective-permute-start | bytes 196616 | tf_op jit(solution)/shard_map/ppermute | solution.py:222
  83.3 3.2 %collective-permute-done.9 = bf16[16,2048]{1,0:T(8,128)(2,1)S(1)} collective-permute-done((bf16[16,2048]{1,0:T(8,128)(2,1)S(1)}, bf16[16,2048]{1,0:T(8,128)(2,1)S(1)}, u32[]{:S(2)}, u32[]{:S(2)}) %collective-permute-start.9) | collective-permute-done | bytes 65568 | tf_op jit(solution)/shard_map/ppermute | solution.py:222
  86.6 1.1 %shard_map.114 = (bf16[128,1024]{1,0:T(8,128)(2,1)}, bf16[128,1024]{1,0:T(8,128)(2,1)}, bf16[128,1024]{1,0:T(8,128)(2,1)}, f32[16,1024]{1,0:T(8,128)}) custom-call(bf16[8,400,128]{2,1,0:T(8,128)(2,1)S(1)} %all-to-all-done.2.back_ref), custom_call_target="tpu_custom_call" | custom-call | bytes 1671168 | tf_op jit(solution)/shard_map/pallas_call | solution.py:286
  87.8 0.7 convert_add_fusion
  (36 shorter events, 1.6 us)
Async XLA Ops:
  0.6 27.7 %copy-start = (bf16[16,4096]{1,0:T(8,128)(2,1)S(1)}, bf16[16,4096]{1,0:T(8,128)(2,1)}, u32[]{:S(2)}) copy-start(bf16[16,4096]{1,0:T(8,128)(2,1)} %param.13) | copy-start | bytes 393220
  0.6 10.0 %copy-start.1 = (bf16[128,2048]{1,0:T(8,128)(2,1)S(1)}, bf16[128,2048]{1,0:T(8,128)(2,1)}, u32[]{:S(2)}) copy-start(bf16[128,2048]{1,0:T(8,128)(2,1)} %param.10) | copy-start | bytes 1572868
  2.8 25.3 %all-to-all-start = ((bf16[8,384,128]{2,1,0:T(8,128)(2,1)}), bf16[8,384,128]{2,1,0:T(8,128)(2,1)S(1)}, u32[]{:S(2)}, u32[]{:S(2)}) async-start(bf16[8,384,128]{2,1,0:T(8,128)(2,1)} %shard_map.110), calls=%async_computation | async-start | bytes 1572864 | tf_op jit(solution)/shard_map/all_to_all | solution.py:347
  10.7 3.4 %collective-permute-start.1 = (bf16[128,2048]{1,0:T(8,128)(2,1)S(1)}, bf16[128,2048]{1,0:T(8,128)(2,1)S(1)}, u32[]{:S(2)}, u32[]{:S(2)}) collective-permute-start(bf16[128,2048]{1,0:T(8,128)(2,1)S(1)} %copy-done.1), channel_id=1, source_target_pairs={{0,0},{1,2},{2,1},{3,3},{4,4},{5,6},{6,5},{7,7},{8,8},{9,10},{10,9... | collective-permute-start | bytes 1572872 | tf_op jit(solution)/shard_map/ppermute | solution.py:369
  11.3 14.4 %collective-permute-start.2 = (bf16[128,2048]{1,0:T(8,128)(2,1)S(1)}, bf16[128,2048]{1,0:T(8,128)(2,1)S(1)}, u32[]{:S(2)}, u32[]{:S(2)}) collective-permute-start(bf16[128,2048]{1,0:T(8,128)(2,1)S(1)} %copy-done.1), channel_id=1, source_target_pairs={{0,2},{1,0},{2,3},{3,1},{4,6},{5,4},{6,7},{7,5},{8,10},{9,8},{10,1... | collective-permute-start | bytes 1572872 | tf_op jit(solution)/shard_map/ppermute | solution.py:369
  28.2 0.8 copy-start.2
  28.2 2.2 %copy-start.3 = (bf16[1024,2048]{1,0:T(8,128)(2,1)S(1)}, bf16[1024,2048]{1,0:T(8,128)(2,1)}, u32[]{:S(2)}) copy-start(bf16[1024,2048]{1,0:T(8,128)(2,1)} %param.11) | copy-start | bytes 12582916
  28.2 3.7 %collective-permute-start = (bf16[8,256,128]{2,1,0:T(8,128)(2,1)S(1)}, bf16[8,256,128]{2,1,0:T(8,128)(2,1)S(1)}, u32[]{:S(2)}, u32[]{:S(2)}) collective-permute-start(bf16[8,256,128]{2,1,0:T(8,128)(2,1)S(1)} %slice.16), channel_id=1, source_target_pairs={{0,1},{1,0},{2,3},{3,2},{4,5},{5,4},{6,7},{7,6},{8,9},{9,8},{10,11... | collective-permute-start | bytes 1572872 | tf_op jit(solution)/shard_map/ppermute | solution.py:354
  31.8 4.3 %collective-permute-start.3 = (bf16[1040,128]{1,0:T(8,128)(2,1)S(1)}, bf16[1040,128]{1,0:T(8,128)(2,1)S(1)}, u32[]{:S(2)}, u32[]{:S(2)}) collective-permute-start(bf16[1040,128]{1,0:T(8,128)(2,1)S(1)} %get-tuple-element.39), channel_id=1, source_target_pairs={{0,1},{1,0},{2,3},{3,2},{4,5},{5,4},{6,7},{7,6},{8,9},{9,8},{10,11... | collective-permute-start | bytes 798728 | tf_op jit(solution)/shard_map/ppermute | solution.py:354
  55.9 4.9 %collective-permute-start.4 = (bf16[8,256,128]{2,1,0:T(8,128)(2,1)S(1)}, bf16[8,256,128]{2,1,0:T(8,128)(2,1)S(1)}, u32[]{:S(2)}, u32[]{:S(2)}) collective-permute-start(bf16[8,256,128]{2,1,0:T(8,128)(2,1)S(1)} %get-tuple-element.31), channel_id=1, source_target_pairs={{0,1},{1,0},{2,3},{3,2},{4,5},{5,4},{6,7},{7,6},{8,9},{9,8},{10,11... | collective-permute-start | bytes 1572872 | tf_op jit(solution)/shard_map/ppermute | solution.py:354
  56.0 3.7 %collective-permute-start.6 = (f32[16,128]{1,0:T(8,128)S(1)}, f32[16,128]{1,0:T(8,128)S(1)}, u32[]{:S(2)}, u32[]{:S(2)}) collective-permute-start(f32[16,128]{1,0:T(8,128)S(1)} %convert_reduce_fusion), channel_id=1, source_target_pairs={{0,2},{2,0},{1,3},{3,1},{4,6},{6,4},{5,7},{7,5},{8,10},{10,8},{9,1... | collective-permute-start | bytes 24584 | tf_op jit(solution)/shard_map/ppermute | solution.py:429
  57.4 3.4 %collective-permute-start.5 = (f32[16,128]{1,0:T(8,128)S(1)}, f32[16,128]{1,0:T(8,128)S(1)}, u32[]{:S(2)}, u32[]{:S(2)}) collective-permute-start(f32[16,128]{1,0:T(8,128)S(1)} %get-tuple-element.33), channel_id=1, source_target_pairs={{0,1},{1,0},{2,3},{3,2},{4,5},{5,4},{6,7},{7,6},{8,9},{9,8},{10,11... | collective-permute-start | bytes 24584 | tf_op jit(solution)/shard_map/ppermute | solution.py:354
  59.9 6.9 %collective-permute-start.7 = (bf16[16,2048]{1,0:T(8,128)(2,1)S(1)}, bf16[16,2048]{1,0:T(8,128)(2,1)S(1)}, u32[]{:S(2)}, u32[]{:S(2)}) collective-permute-start(bf16[16,2048]{1,0:T(8,128)(2,1)S(1)} %fusion), channel_id=1, source_target_pairs={{0,4},{4,0},{8,12},{12,8},{16,20},{20,16},{24,28},{28,24},{1,5},{5... | collective-permute-start | bytes 196616 | tf_op jit(solution)/shard_map/ppermute | solution.py:222
  62.0 24.5 %all-to-all-start.2 = ((bf16[8,400,128]{2,1,0:T(8,128)(2,1)}), bf16[8,400,128]{2,1,0:T(8,128)(2,1)S(1)}, u32[]{:S(2)}, u32[]{:S(2)}) async-start(bf16[8,400,128]{2,1,0:T(8,128)(2,1)} %pad_maximum_fusion), calls=%async_computation.2 | async-start | bytes 1638400 | tf_op jit(solution)/shard_map/all_to_all | solution.py:347
  66.8 14.0 %collective-permute-start.8 = (bf16[16,2048]{1,0:T(8,128)(2,1)S(1)}, bf16[16,2048]{1,0:T(8,128)(2,1)S(1)}, u32[]{:S(2)}, u32[]{:S(2)}) collective-permute-start(bf16[16,2048]{1,0:T(8,128)(2,1)S(1)} %add_convert_fusion.2), channel_id=1, source_target_pairs={{0,8},{4,12},{8,0},{12,4},{16,24},{20,28},{24,16},{28,20},{1,9},{5... | collective-permute-start | bytes 196616 | tf_op jit(solution)/shard_map/ppermute | solution.py:222
  80.8 5.7 %collective-permute-start.9 = (bf16[16,2048]{1,0:T(8,128)(2,1)S(1)}, bf16[16,2048]{1,0:T(8,128)(2,1)S(1)}, u32[]{:S(2)}, u32[]{:S(2)}) collective-permute-start(bf16[16,2048]{1,0:T(8,128)(2,1)S(1)} %add_convert_fusion.1), channel_id=1, source_target_pairs={{0,16},{4,20},{8,24},{12,28},{16,0},{20,4},{24,8},{28,12},{1,17},{... | collective-permute-start | bytes 196616 | tf_op jit(solution)/shard_map/ppermute | solution.py:222
  86.5 1.3 %collective-permute-start.10 = (bf16[16,2048]{1,0:T(8,128)(2,1)S(1)}, bf16[16,2048]{1,0:T(8,128)(2,1)S(1)}, u32[]{:S(2)}, u32[]{:S(2)}) collective-permute-start(bf16[16,2048]{1,0:T(8,128)(2,1)S(1)} %convert_add_fusion.1), channel_id=1, source_target_pairs={{0,1},{1,0},{2,3},{3,2},{4,5},{5,4},{6,7},{7,6},{8,9},{9,8},{10,11... | collective-permute-start | bytes 196616 | tf_op jit(solution)/shard_map/ppermute | solution.py:222
